TPU v7x, 32 devices: a whole 2x2x4 slice. The times are simulated.
32 devices in a mesh: patch: 2 (over y), tile: 8 (over z, core), row: 2 (over x), band: 1.
Axes of the slice: x: 2, y: 2, z: 4, core: 2. Of those that a mesh axis runs over, the one named last changes fastest.
Arguments:
- stamps: bfloat16 [768, 64, 128], P(('patch', 'tile', 'row', 'band')), parts along dimension 0, may hold values from -6 to 6
- variance: bfloat16 [768, 64, 128], P(('patch', 'tile', 'row', 'band')), parts along dimension 0, may hold values from 0.25 to 4
- basis_v: bfloat16 [21, 41], replicated, may hold values from -1 to 1
- basis_u: bfloat16 [21, 41], replicated, may hold values from -1 to 1
- coefficients: float32 [800, 21], P('patch'), parts along dimension 0, may hold values from 0.03 to 0.3
- coef_index: int32 [768], P(('patch', 'tile', 'row', 'band')), parts along dimension 0, may hold values from 0 to 399
- tile_dest: int32 [768], P(('patch', 'tile', 'row', 'band')), parts along dimension 0, may hold values from 0 to 7, as said below
- row_offset: int32 [768], P(('patch', 'tile', 'row', 'band')), parts along dimension 0, may hold values from 0 to 448
- sub_pixel: int32 [768, 2], P(('patch', 'tile', 'row', 'band')), parts along dimension 0, may hold values from 0 to 63
Outputs:
- coadd: float32 [8192, 128], P(('patch', 'tile', 'row', 'band')), parts along dimension 0
There are 2 independent parts, one for each index of `patch`. A program takes and returns all parts, laid end to end along the dimension named above; an argument that names none is the same for every part. Nothing has to cross between parts.
Inputs may be any that keep to these rules, and one draw needn't show every extreme that they name: `tile_dest`: among the 24 stamps of one device at most 3 name the same tile, and one tile is named by exactly 3 stamps of every device.
All inputs are finite; a program needn't handle non-finite values.
Results may differ from a plain program's by a relative error of at most 0.0055.
Values may be sent and summed in bfloat16 or wider, within the bound.
A program may use at most 64 MiB of HBM per device.

v0:
```python
import math

import jax
import jax.numpy as jnp
from jax import lax
from jax.sharding import PartitionSpec as P

SUBSTEPS = 64
TILE_ROWS = 512


def band_tables(basis_v, basis_u, stamp_rows, stamp_cols):
    tap_count = basis_v.shape[1]
    half_width = (tap_count - 1) // 2
    row_ids = jnp.arange(stamp_rows)
    col_ids = jnp.arange(stamp_cols)
    tap_ids = jnp.arange(tap_count)
    lag_rows = row_ids[None, :] - row_ids[:, None] + half_width
    pick_rows = (lag_rows[None, :, :] == tap_ids[:, None, None]).astype(jnp.bfloat16)
    vertical = jnp.einsum(
        "ka,aij->kij", basis_v, pick_rows, preferred_element_type=jnp.float32
    ).astype(jnp.bfloat16)
    lag_cols = col_ids[:, None] - col_ids[None, :] + half_width
    pick_cols = (lag_cols[None, :, :] == tap_ids[:, None, None]).astype(jnp.bfloat16)
    horizontal = jnp.einsum(
        "ka,apq->pkq", basis_u, pick_cols, preferred_element_type=jnp.float32
    ).astype(jnp.bfloat16)
    return (vertical, horizontal.reshape(stamp_cols, -1))


def coef_rows(coefficients, indices):
    picks = (indices[:, None] == jnp.arange(coefficients.shape[0])[None, :]).astype(jnp.float32)
    return jnp.dot(picks, coefficients, precision=lax.Precision.HIGHEST)


def match_stamps(images, coef_part, vertical, horiz_table):
    slot_count, stamp_rows, stamp_cols = images.shape
    nbasis = vertical.shape[0]
    group_size = math.gcd(slot_count, 4)

    def one_group(operands):
        group_images, group_coef = operands
        flattened = group_images.reshape(group_size * stamp_rows, stamp_cols)
        horizontal = jnp.dot(flattened, horiz_table, preferred_element_type=jnp.float32).astype(
            jnp.bfloat16
        )
        horizontal = horizontal.reshape(group_size, stamp_rows, nbasis, stamp_cols)
        vertical_out = jnp.einsum(
            "kai,bikc->bkac", vertical, horizontal, preferred_element_type=jnp.float32
        )
        combined = jnp.sum(group_coef[:, :, None, None] * vertical_out, axis=1)
        return combined.astype(jnp.bfloat16)

    grouped = (
        images.reshape(slot_count // group_size, group_size, stamp_rows, stamp_cols),
        coef_part.reshape(slot_count // group_size, group_size, nbasis),
    )
    return lax.map(one_group, grouped).reshape(slot_count, stamp_rows, stamp_cols)


def bilinear(values, frac_rows, frac_cols):
    below = jnp.concatenate([values[:, 1:], values[:, -1:]], axis=1)
    mixed = (1.0 - frac_rows) * values + frac_rows * below
    beside = jnp.concatenate([mixed[:, :, 1:], mixed[:, :, -1:]], axis=2)
    return (1.0 - frac_cols) * mixed + frac_cols * beside


def contributions(matched, spreads, details):
    live = (details[:, 0] > 0)[:, None, None]
    frac_rows = details[:, 2].astype(jnp.float32)[:, None, None] / SUBSTEPS
    frac_cols = details[:, 3].astype(jnp.float32)[:, None, None] / SUBSTEPS
    warped = bilinear(matched.astype(jnp.float32), frac_rows, frac_cols)
    spread = bilinear(spreads.astype(jnp.float32), frac_rows, frac_cols)
    weight = jnp.where(live, 1.0 / jnp.where(live, spread, 1.0), 0.0)
    rows_at = details[:, 1][:, None] + jnp.arange(matched.shape[1], dtype=jnp.int32)[None, :]
    return (weight * warped, weight, rows_at)


def local(
    stamps, variance, basis_v, basis_u, coefficients, coef_index, tile_dest, row_offset, sub_pixel
):
    tile_count = lax.axis_size("tile")
    local_count, stamp_rows, stamp_cols = stamps.shape
    capacity = max(2, (local_count + tile_count - 1) // tile_count)
    slot_total = tile_count * capacity
    vertical, horiz_table = band_tables(basis_v, basis_u, stamp_rows, stamp_cols)
    chosen = (tile_dest[:, None] == jnp.arange(tile_count, dtype=jnp.int32)[None, :]).astype(
        jnp.int32
    )
    earlier = jnp.cumsum(chosen, axis=0) - chosen
    ranking = jnp.sum(earlier * chosen, axis=1)
    slot_of = tile_dest * capacity + ranking

    def pack(values):
        empty_buffer = jnp.zeros((slot_total,) + values.shape[1:], values.dtype)
        filled = empty_buffer.at[slot_of].set(values)
        return filled.reshape((tile_count, capacity) + values.shape[1:])

    base_meta = [jnp.ones_like(row_offset), row_offset, sub_pixel[:, 0], sub_pixel[:, 1]]
    matched_here = match_stamps(stamps, coef_rows(coefficients, coef_index), vertical, horiz_table)
    meta_sent = jnp.stack(base_meta, axis=1)
    images = lax.all_to_all(pack(matched_here), "tile", split_axis=0, concat_axis=0, tiled=True)
    spreads = lax.all_to_all(pack(variance), "tile", split_axis=0, concat_axis=0, tiled=True)
    details = lax.all_to_all(pack(meta_sent), "tile", split_axis=0, concat_axis=0, tiled=True)
    leading = images.shape[:2]
    results = contributions(
        images.reshape((-1,) + images.shape[2:]),
        spreads.reshape((-1,) + spreads.shape[2:]),
        details.reshape(-1, details.shape[2]),
    )
    numer, denom, rows_at = tuple((item.reshape(leading + item.shape[1:]) for item in results))
    rows_flat = rows_at.reshape(-1)
    numer_tile = (
        jnp.zeros((TILE_ROWS, stamp_cols), jnp.float32)
        .at[rows_flat]
        .add(numer.reshape(-1, stamp_cols))
    )
    denom_tile = (
        jnp.zeros((TILE_ROWS, stamp_cols), jnp.float32)
        .at[rows_flat]
        .add(denom.reshape(-1, stamp_cols))
    )
    numer_own, denom_own = (
        lax.psum_scatter(numer_tile, ("row", "band"), scatter_dimension=0, tiled=True),
        lax.psum_scatter(denom_tile, ("row", "band"), scatter_dimension=0, tiled=True),
    )
    return numer_own / (denom_own + 1.0)


def solution(mesh):
    in_specs = (
        P(("patch", "tile", "row", "band"), None, None),
        P(("patch", "tile", "row", "band"), None, None),
        P(),
        P(),
        P("patch", None),
        P(("patch", "tile", "row", "band")),
        P(("patch", "tile", "row", "band")),
        P(("patch", "tile", "row", "band")),
        P(("patch", "tile", "row", "band"), None),
    )
    out_specs = P(("patch", "tile", "row", "band"), None)
    return jax.shard_map(local, mesh=mesh, in_specs=in_specs, out_specs=out_specs, check_vma=False)
```

profile of v0, /device:TPU:0, one launch (start us, length us, event | category | flops | bytes accessed | tf_op | source)
XLA Modules:
  0.0 139.0 jit_solution(17910034526923628088)
XLA Ops:
  11.1 6.3 %all-to-all-start = ((s32[8,3,4]{1,2,0:T(4,128)}), s32[8,3,4]{1,2,0:T(4,128)S(1)}, u32[]{:S(2)}, u32[]{:S(2)}) async-start(s32[8,3,4]{1,2,0:T(4,128)} %copy.32), calls=%async_computation | async-start | bytes 32768 | tf_op jit(solution)/shard_map/all_to_all | solution.py:104
  21.9 30.3 %while.10 = (s32[]{:T(128)}, bf16[6,4,64,128]{3,2,1,0:T(8,128)(2,1)S(1)}, f32[6,4,21]{2,1,0:T(4,128)S(1)}, bf16[6,4,64,128]{3,2,1,0:T(8,128)(2,1)}, bf16[128,268...) while((s32[]{:T(128)}, bf16[6,4,64,128]{3,2,1,0:T(8,128)(2,1)S(1)}, f32[6,4,21]{2,1,0:T(4,128)S(1)}, ...), condition=%wide.region_6.7_spmd, body=%wide.region_4.6_spmd.sunk | while | flops 266272768 | bytes 6760169 | solution.py:58
  22.8 1.6 %convolution_convert_fusion.2 = bf16[256,2688]{1,0:T(8,128)(2,1)S(1)} fusion(bf16[256,128]{1,0:T(8,128)(2,1)S(1)} %bitcast.99, bf16[128,2688]{1,0:T(8,128)(2,1)} %get-tuple-element.135), kind=kOutput, calls=%fused_computation.5.clone.1 | convolution fusion | flops 176848896 | bytes 2129920 | tf_op jit(solution)/shard_map/while/body/eval_jaxpr/dot_general | solution.py:44
  25.5 1.5 %fusion.49 = bf16[4,64,128]{2,1,0:T(8,128)(2,1)S(1)} fusion(bf16[4,64,21,128]{3,2,1,0:T(8,128)(2,1)S(1)} %reshape.241, f32[4,21]{0,1:T(8,128)S(1)} %copy.47, bf16[21,64,64]{2,1,0:T(8,128)(2,1)} %get-tuple-element.136), kind=kOutput, calls=%fused_computation.7.clone.1 | convolution fusion | flops 89423872 | bytes 1614160 | tf_op jit(solution)/shard_map/while/body/eval_jaxpr/kai,bikc->bkac/dot_general | solution.py:48
  27.9 1.6 %convolution_convert_fusion.2 = bf16[256,2688]{1,0:T(8,128)(2,1)S(1)} fusion(bf16[256,128]{1,0:T(8,128)(2,1)S(1)} %bitcast.99, bf16[128,2688]{1,0:T(8,128)(2,1)} %get-tuple-element.135), kind=kOutput, calls=%fused_computation.5.clone.1 | convolution fusion | flops 176848896 | bytes 2129920 | tf_op jit(solution)/shard_map/while/body/eval_jaxpr/dot_general | solution.py:44
  30.5 1.5 %fusion.49 = bf16[4,64,128]{2,1,0:T(8,128)(2,1)S(1)} fusion(bf16[4,64,21,128]{3,2,1,0:T(8,128)(2,1)S(1)} %reshape.241, f32[4,21]{0,1:T(8,128)S(1)} %copy.47, bf16[21,64,64]{2,1,0:T(8,128)(2,1)} %get-tuple-element.136), kind=kOutput, calls=%fused_computation.7.clone.1 | convolution fusion | flops 89423872 | bytes 1614160 | tf_op jit(solution)/shard_map/while/body/eval_jaxpr/kai,bikc->bkac/dot_general | solution.py:48
  32.9 1.6 %convolution_convert_fusion.2 = bf16[256,2688]{1,0:T(8,128)(2,1)S(1)} fusion(bf16[256,128]{1,0:T(8,128)(2,1)S(1)} %bitcast.99, bf16[128,2688]{1,0:T(8,128)(2,1)} %get-tuple-element.135), kind=kOutput, calls=%fused_computation.5.clone.1 | convolution fusion | flops 176848896 | bytes 2129920 | tf_op jit(solution)/shard_map/while/body/eval_jaxpr/dot_general | solution.py:44
  35.6 1.5 %fusion.49 = bf16[4,64,128]{2,1,0:T(8,128)(2,1)S(1)} fusion(bf16[4,64,21,128]{3,2,1,0:T(8,128)(2,1)S(1)} %reshape.241, f32[4,21]{0,1:T(8,128)S(1)} %copy.47, bf16[21,64,64]{2,1,0:T(8,128)(2,1)} %get-tuple-element.136), kind=kOutput, calls=%fused_computation.7.clone.1 | convolution fusion | flops 89423872 | bytes 1614160 | tf_op jit(solution)/shard_map/while/body/eval_jaxpr/kai,bikc->bkac/dot_general | solution.py:48
  38.0 1.6 %convolution_convert_fusion.2 = bf16[256,2688]{1,0:T(8,128)(2,1)S(1)} fusion(bf16[256,128]{1,0:T(8,128)(2,1)S(1)} %bitcast.99, bf16[128,2688]{1,0:T(8,128)(2,1)} %get-tuple-element.135), kind=kOutput, calls=%fused_computation.5.clone.1 | convolution fusion | flops 176848896 | bytes 2129920 | tf_op jit(solution)/shard_map/while/body/eval_jaxpr/dot_general | solution.py:44
  40.6 1.5 %fusion.49 = bf16[4,64,128]{2,1,0:T(8,128)(2,1)S(1)} fusion(bf16[4,64,21,128]{3,2,1,0:T(8,128)(2,1)S(1)} %reshape.241, f32[4,21]{0,1:T(8,128)S(1)} %copy.47, bf16[21,64,64]{2,1,0:T(8,128)(2,1)} %get-tuple-element.136), kind=kOutput, calls=%fused_computation.7.clone.1 | convolution fusion | flops 89423872 | bytes 1614160 | tf_op jit(solution)/shard_map/while/body/eval_jaxpr/kai,bikc->bkac/dot_general | solution.py:48
  43.0 1.6 %convolution_convert_fusion.2 = bf16[256,2688]{1,0:T(8,128)(2,1)S(1)} fusion(bf16[256,128]{1,0:T(8,128)(2,1)S(1)} %bitcast.99, bf16[128,2688]{1,0:T(8,128)(2,1)} %get-tuple-element.135), kind=kOutput, calls=%fused_computation.5.clone.1 | convolution fusion | flops 176848896 | bytes 2129920 | tf_op jit(solution)/shard_map/while/body/eval_jaxpr/dot_general | solution.py:44
  45.7 1.5 %fusion.49 = bf16[4,64,128]{2,1,0:T(8,128)(2,1)S(1)} fusion(bf16[4,64,21,128]{3,2,1,0:T(8,128)(2,1)S(1)} %reshape.241, f32[4,21]{0,1:T(8,128)S(1)} %copy.47, bf16[21,64,64]{2,1,0:T(8,128)(2,1)} %get-tuple-element.136), kind=kOutput, calls=%fused_computation.7.clone.1 | convolution fusion | flops 89423872 | bytes 1614160 | tf_op jit(solution)/shard_map/while/body/eval_jaxpr/kai,bikc->bkac/dot_general | solution.py:48
  48.0 1.6 %convolution_convert_fusion.2 = bf16[256,2688]{1,0:T(8,128)(2,1)S(1)} fusion(bf16[256,128]{1,0:T(8,128)(2,1)S(1)} %bitcast.99, bf16[128,2688]{1,0:T(8,128)(2,1)} %get-tuple-element.135), kind=kOutput, calls=%fused_computation.5.clone.1 | convolution fusion | flops 176848896 | bytes 2129920 | tf_op jit(solution)/shard_map/while/body/eval_jaxpr/dot_general | solution.py:44
  53.1 4.4 %scatter_fusion.1 = bf16[24,64,128]{2,1,0:T(8,128)(2,1)} fusion(bf16[24,64,128]{2,1,0:T(8,128)(2,1)} %broadcast.157.clone, s32[24]{0:T(128)S(1)} %compare_select_fusion.1, bf16[24,64,128]{2,1,0:T(8,128)(2,1)S(1)} %bitcast.105), kind=kCustom, calls=%fused_computation.2 | custom fusion | bytes 1179744 | tf_op jit(solution)/shard_map/scatter | solution.py:96
  57.4 5.1 %all-to-all-start.2 = ((bf16[8,3,64,128]{3,2,1,0:T(8,128)(2,1)}), bf16[8,3,64,128]{3,2,1,0:T(8,128)(2,1)S(1)}, u32[]{:S(2)}, u32[]{:S(2)}) async-start(bf16[8,3,64,128]{3,2,1,0:T(8,128)(2,1)} %bitcast.25), calls=%async_computation.2 | async-start | bytes 786432 | tf_op jit(solution)/shard_map/all_to_all | solution.py:102
  63.4 4.4 %scatter_fusion = bf16[24,64,128]{2,1,0:T(8,128)(2,1)} fusion(bf16[24,64,128]{2,1,0:T(8,128)(2,1)} %broadcast.157.clone.1, s32[24]{0:T(128)S(1)} %compare_select_fusion.1, bf16[24,64,128]{2,1,0:T(8,128)(2,1)S(1)} %copy-done.1), kind=kCustom, calls=%fused_computation.1 | custom fusion | bytes 1179744 | tf_op jit(solution)/shard_map/scatter | solution.py:96
  68.4 6.7 %all-to-all-done.2 = bf16[8,3,64,128]{3,2,1,0:T(8,128)(2,1)S(1)} async-done(((bf16[8,3,64,128]{3,2,1,0:T(8,128)(2,1)}), bf16[8,3,64,128]{3,2,1,0:T(8,128)(2,1)S(1)}, u32[]{:S(2)}, u32[]{:S(2)}) %all-to-all-start.2) | async-done | bytes 393248 | tf_op jit(solution)/shard_map/all_to_all | solution.py:102
  75.1 3.5 %all-to-all-start.1 = ((bf16[8,3,64,128]{3,2,1,0:T(8,128)(2,1)}), bf16[8,3,64,128]{3,2,1,0:T(8,128)(2,1)S(1)}, u32[]{:S(2)}, u32[]{:S(2)}) async-start(bf16[8,3,64,128]{3,2,1,0:T(8,128)(2,1)} %bitcast.11), calls=%async_computation.1 | async-start | bytes 786432 | tf_op jit(solution)/shard_map/all_to_all | solution.py:103
  79.1 11.9 %all-to-all-done.1 = bf16[8,3,64,128]{3,2,1,0:T(8,128)(2,1)S(1)} async-done(((bf16[8,3,64,128]{3,2,1,0:T(8,128)(2,1)}), bf16[8,3,64,128]{3,2,1,0:T(8,128)(2,1)S(1)}, u32[]{:S(2)}, u32[]{:S(2)}) %all-to-all-start.1) | async-done | bytes 393248 | tf_op jit(solution)/shard_map/all_to_all | solution.py:103
  93.5 1.7 %fusion.21 = (f32[1536,128]{1,0:T(8,128)S(1)}, f32[1536,128]{1,0:T(8,128)S(1)}) fusion(f32[24,64,128]{2,1,0:T(8,128)S(1)} %get-tuple-element.69, f32[1536]{0:T(1024)S(1)} %mul.126, f32[1536]{0:T(1024)S(1)} %mul.122, f32[1536]{0:T(1024)S(1)} %mul.119, bf16[8,3,64,128]{3,2,1,0:T(8,128)(2,1)S(1)} %all-to-all-done.2, f32[1536,1]{1,0:T(8,128)S(1)} %bitcast.101, ...), kind=kLoop, calls=%fused_computation.37 | loop fusion | flops 3145728 | bytes 4744704 | tf_op jit(solution)/shard_map/mul | solution.py:65
  95.2 10.6 %scatter_custom_fusion.3 = f32[512,128]{1,0:T(8,128)} fusion(s32[1536]{0:T(1024)S(1)} %fusion.32, f32[1536,128]{1,0:T(8,128)S(1)} %get-tuple-element.73, f32[1536,128]{1,0:T(8,128)S(1)} %get-tuple-element.72, f32[1536,1]{1,0:T(8,128)} %bitcast.103, f32[]{:T(128)} %constant.55, f32[1536,127]{1,0:T(8,128)S(1)} %bitcast.102, f32[1536]{0:T(1024)S(1)} %mul.131, ...), kind=kCustom, calls=%fused_computation.32 | custom fusion | flops 983040 | bytes 2635784 | tf_op jit(solution)/shard_map/scatter-add | solution.py:116
  105.9 9.4 %scatter_custom_fusion.4 = f32[512,128]{1,0:T(8,128)} fusion(s32[1536]{0:T(1024)S(1)} %fusion.32, f32[1536,128]{1,0:T(8,128)S(1)} %get-tuple-element.73, f32[]{:T(128)} %constant.18.clone.1), kind=kCustom, calls=%fused_computation.48 | custom fusion | flops 196608 | bytes 262148 | tf_op jit(solution)/shard_map/scatter-add | solution.py:121
  116.5 14.0 %reduce-scatter.5.cloned.1.call-done = f32[256,128]{1,0:T(8,128)} async-done(((f32[512,128]{1,0:T(8,128)}), f32[256,128]{1,0:T(8,128)}) %reduce-scatter.5.cloned.1.call-update) | async-done | bytes 131088 | tf_op jit(solution)/shard_map/reduce_scatter | solution.py:125
  130.5 1.6 %add_divide_fusion = f32[256,128]{1,0:T(8,128)} fusion(f32[256,128]{1,0:T(8,128)} %reduce-scatter.3.cloned.1.call-done, f32[256,128]{1,0:T(8,128)} %reduce-scatter.5.cloned.1.call-done), kind=kLoop, calls=%fused_computation.47 | loop fusion | flops 65536 | bytes 393216 | tf_op jit(solution)/shard_map/div | solution.py:127
  (94 shorter events, 28.4 us)
Async XLA Ops:
  6.5 15.2 %copy-start = (f32[400,21]{0,1:T(8,128)S(1)}, f32[400,21]{0,1:T(8,128)}, u32[]{:S(2)}) copy-start(f32[400,21]{0,1:T(8,128)} %param.15) | copy-start | bytes 100804
  11.1 46.4 %all-to-all-start = ((s32[8,3,4]{1,2,0:T(4,128)}), s32[8,3,4]{1,2,0:T(4,128)S(1)}, u32[]{:S(2)}, u32[]{:S(2)}) async-start(s32[8,3,4]{1,2,0:T(4,128)} %copy.32), calls=%async_computation | async-start | bytes 32768 | tf_op jit(solution)/shard_map/all_to_all | solution.py:104
  18.9 1.7 %copy-start.2 = (bf16[21,41]{1,0:T(8,128)(2,1)S(1)}, bf16[21,41]{1,0:T(8,128)(2,1)}, u32[]{:S(2)}) copy-start(bf16[21,41]{1,0:T(8,128)(2,1)} %param.13) | copy-start | bytes 5170
  19.4 2.4 %copy-start.3 = (s32[24]{0:T(128)S(1)}, s32[24]{0:T(128)}, u32[]{:S(2)}) copy-start(s32[24]{0:T(128)} %param.16) | copy-start | bytes 292
  52.2 11.1 %copy-start.1 = (bf16[24,64,128]{2,1,0:T(8,128)(2,1)S(1)}, bf16[24,64,128]{2,1,0:T(8,128)(2,1)}, u32[]{:S(2)}) copy-start(bf16[24,64,128]{2,1,0:T(8,128)(2,1)} %param.12) | copy-start | bytes 1179652
  57.4 17.7 %all-to-all-start.2 = ((bf16[8,3,64,128]{3,2,1,0:T(8,128)(2,1)}), bf16[8,3,64,128]{3,2,1,0:T(8,128)(2,1)S(1)}, u32[]{:S(2)}, u32[]{:S(2)}) async-start(bf16[8,3,64,128]{3,2,1,0:T(8,128)(2,1)} %bitcast.25), calls=%async_computation.2 | async-start | bytes 786432 | tf_op jit(solution)/shard_map/all_to_all | solution.py:102
  75.1 15.9 %all-to-all-start.1 = ((bf16[8,3,64,128]{3,2,1,0:T(8,128)(2,1)}), bf16[8,3,64,128]{3,2,1,0:T(8,128)(2,1)S(1)}, u32[]{:S(2)}, u32[]{:S(2)}) async-start(bf16[8,3,64,128]{3,2,1,0:T(8,128)(2,1)} %bitcast.11), calls=%async_computation.1 | async-start | bytes 786432 | tf_op jit(solution)/shard_map/all_to_all | solution.py:103
  78.6 37.9 %reduce-scatter.3.cloned.1.call-start = ((), (), s32[]{:S(2)}) async-start(), calls=%async_computation.5 | async-start | bytes 393216 | tf_op jit(solution)/shard_map/reduce_scatter | solution.py:124
  105.8 24.7 %reduce-scatter.5.cloned.1.call-start = ((), (), s32[]{:S(2)}) async-start(), calls=%async_computation.6 | async-start | bytes 393216 | tf_op jit(solution)/shard_map/reduce_scatter | solution.py:125
Sparse Core Ops, SparseCore 0:
  105.9 10.5 reduce-scatter.2
  118.8 11.6 reduce-scatter.4
where the time goes:
time: 141 us; the launch traced here: 139 us
  waiting for transfers between devices  33.9 us (24%)
  local copies, waits for them, and re-layouts  28.8 us (20%)
  other arithmetic  26.9 us (19%)
  matrix products  20.6 us (15%)
  starting transfers between devices  15 us (11%)
  between operations  13.6 us (10%)
    reduce_scatter x1, waiting for transfers between devices, local(): lax.psum_scatter(denom_tile, ('row', 'band'), scatter_dimension=0, tiled=...  14 us
    all_to_all x1, waiting for transfers between devices, local(): lax.all_to_all(pack(variance), 'tile', split_axis=0, concat_axis=0, tiled...  11.9 us
    scatter-add x1, other arithmetic, local(): numer_tile = jnp.zeros((TILE_ROWS, stamp_cols), jnp.float32).at[rows_flat...  10.6 us
    dot_general x6, matrix products, one_group(): jnp.dot(flattened, horiz_table, preferred_element_type=jnp.float32)  9.64 us
    scatter-add x1, other arithmetic, local(): denom_tile = jnp.zeros((TILE_ROWS, stamp_cols), jnp.float32).at[rows_flat...  9.4 us
    scatter x3, local copies, waits for them, and re-layouts, pack(): filled = empty_buffer.at[slot_of].set(values)  9.36 us
    dot_general x6, matrix products, one_group(): jnp.einsum('kai,bikc->bkac', vertical, horizontal, preferred_element_type...  8.98 us
    all_to_all x1, waiting for transfers between devices, local(): lax.all_to_all(pack(matched_here), 'tile', split_axis=0, concat_axis=0, t...  6.67 us
  transfers between devices with their start and end apart: 5, of which 4 were waited for; matrix products, arithmetic and copies ran while one was open for 40% of the time, Pallas kernels for 0%

commit v1 on v0

v1 whole, which is shorter than its diff:
```python
import functools

import jax
import jax.numpy as jnp
from jax import lax
from jax.experimental import pallas as pl
from jax.experimental.pallas import tpu as pltpu
from jax.sharding import PartitionSpec as P

SUBSTEPS = 64
TILE_ROWS = 512
MESH = pl.DeviceIdType.MESH


def largest_divisor(value, limit):
    return max(d for d in range(1, limit + 1) if value % d == 0)


def paired(index, step, count):
    if count & (count - 1):
        return lax.rem(index + step, count)
    total, bit = 0, 1
    while bit < count:
        digit = lax.rem(lax.div(index, bit), 2) + lax.rem(lax.div(step, bit), 2)
        total = total + lax.rem(digit, 2) * bit
        bit *= 2
    return total


def kernel(
    sizes,
    stamps, variance, basis_v, basis_u, coef, coef_index, tile_dest, row_offset, sub_pixel,
    out,
    taps_v, taps_u, vtab, utab, tmat, send_x, send_m, recv_x, recv_m, acc, part_s, part_r,
    sx_sem, rx_sem, sm_sem, rm_sem, sp_sem, rp_sem,
):
    tiles, rows_n, bands, cap = sizes
    count, sh, sw = stamps.shape
    nb, tap_count = basis_v.shape
    half = (tap_count - 1) // 2
    owners = rows_n * bands
    own_rows = TILE_ROWS // owners
    me = lax.axis_index("tile")
    mine = lax.axis_index("row") * bands + lax.axis_index("band")

    def owner_id(q):
        peer = lax.rem(mine + q, owners)
        return peer, {"row": lax.div(peer, bands), "band": lax.rem(peer, bands)}

    barrier = pltpu.get_barrier_semaphore()
    for step in range(1, tiles):
        pl.semaphore_signal(
            barrier, inc=1, device_id={"tile": lax.rem(me + step, tiles)}, device_id_type=MESH
        )
    for q in range(1, owners):
        pl.semaphore_signal(barrier, inc=1, device_id=owner_id(q)[1], device_id_type=MESH)

    taps_v[...] = jnp.zeros_like(taps_v)
    taps_u[...] = jnp.zeros_like(taps_u)
    taps_v[0:nb, 0:tap_count] = basis_v[...].astype(jnp.float32)
    taps_u[0:nb, 0:tap_count] = basis_u[...].astype(jnp.float32)
    taps_v[...] = pltpu.roll(taps_v[...], sw - half, 1)
    taps_u[...] = pltpu.roll(taps_u[...], sw - half, 1)
    lag = lax.broadcasted_iota(jnp.int32, (sw, sw), 1) - lax.broadcasted_iota(jnp.int32, (sw, sw), 0)
    near = jnp.abs(lag) <= half
    for k in range(nb):
        line = jnp.broadcast_to(taps_v[k : k + 1, :], (sh, sw))
        rolled = pltpu.roll(line, 0, 1, stride=1, stride_axis=0)
        vtab[k * sh : (k + 1) * sh, :] = rolled[:, :sh].astype(jnp.bfloat16)
        line = jnp.broadcast_to(taps_u[k : k + 1, :], (sw, sw))
        rolled = pltpu.roll(line, 0, 1, stride=1, stride_axis=0)
        utab[k * sw : (k + 1) * sw, :] = jnp.where(near, rolled, 0.0).T.astype(jnp.bfloat16)

    pl.semaphore_wait(barrier, tiles - 1 + owners - 1)

    last_row = lax.broadcasted_iota(jnp.int32, (sh, sw), 0) == sh - 1
    last_col = lax.broadcasted_iota(jnp.int32, (sh, sw), 1) == sw - 1
    width = send_m.shape[2]
    lane = lax.broadcasted_iota(jnp.int32, (1, width), 1)
    chunk = largest_divisor(nb, 7)

    def bilinear(values, frac_rows, frac_cols):
        below = jnp.where(last_row, values, pltpu.roll(values, sh - 1, 0))
        mixed = (1.0 - frac_rows) * values + frac_rows * below
        beside = jnp.where(last_col, mixed, pltpu.roll(mixed, sw - 1, 1))
        return (1.0 - frac_cols) * mixed + frac_cols * beside

    def data_copy(step):
        return pltpu.make_async_remote_copy(
            src_ref=send_x.at[step], dst_ref=recv_x.at[step],
            send_sem=sx_sem.at[step], recv_sem=rx_sem.at[step],
            device_id={"tile": paired(me, step, tiles)}, device_id_type=MESH,
        )

    def place_copy(step):
        return pltpu.make_async_remote_copy(
            src_ref=send_m.at[step], dst_ref=recv_m.at[step],
            send_sem=sm_sem.at[step], recv_sem=rm_sem.at[step],
            device_id={"tile": paired(me, step, tiles)}, device_id_type=MESH,
        )

    def produce(step):
        dst = paired(me, step, tiles)
        listed = jnp.int32(0)
        for s in range(count):
            listed = jnp.where(tile_dest[s] == dst, listed * (count + 1) + (s + 1), listed)
        picks, live = [], []
        for r in range(cap):
            digit = lax.rem(listed, count + 1)
            listed = lax.div(listed, count + 1)
            picks.append(jnp.maximum(digit - 1, 0))
            live.append(digit > 0)
        images = jnp.concatenate([stamps[p] for p in picks], axis=1)
        weights = [coef[pl.ds(coef_index[p], 1), :] for p in picks]
        for base in range(0, nb, chunk):
            part = jnp.dot(
                vtab[base * sh : (base + chunk) * sh, :], images, preferred_element_type=jnp.float32
            )
            for k in range(chunk):
                for r in range(cap):
                    block = part[k * sh : (k + 1) * sh, r * sw : (r + 1) * sw]
                    scale = weights[r][:, base + k : base + k + 1]
                    tmat[r * sh : (r + 1) * sh, (base + k) * sw : (base + k + 1) * sw] = (
                        block * scale
                    ).astype(jnp.bfloat16)
        matched = jnp.dot(tmat[...], utab[...], preferred_element_type=jnp.float32)
        matched = matched.astype(jnp.bfloat16).astype(jnp.float32)
        place = jnp.full((1, width), -1, jnp.int32)
        for r in range(cap):
            p = picks[r]
            frac_rows = sub_pixel[p, 0].astype(jnp.float32) * (1.0 / SUBSTEPS)
            frac_cols = sub_pixel[p, 1].astype(jnp.float32) * (1.0 / SUBSTEPS)
            warped = bilinear(matched[r * sh : (r + 1) * sh, :], frac_rows, frac_cols)
            spread = bilinear(variance[p].astype(jnp.float32), frac_rows, frac_cols)
            weight = 1.0 / spread
            send_x[step, r * sh : (r + 1) * sh, 0:sw] = (weight * warped).astype(jnp.bfloat16)
            send_x[step, r * sh : (r + 1) * sh, sw : 2 * sw] = weight.astype(jnp.bfloat16)
            first = jnp.where(live[r], row_offset[p], -4 * TILE_ROWS)
            inside = (lane >= r * sh) & (lane < (r + 1) * sh)
            place = jnp.where(inside, first + lane - r * sh, place)
        send_m[step] = place

    def send_one(i, carry):
        step = tiles - 1 - i
        produce(step)
        data_copy(step).start()
        place_copy(step).start()
        return carry

    lax.fori_loop(0, tiles - 1, send_one, 0)
    produce(0)

    row_ids = lax.broadcasted_iota(jnp.int32, (TILE_ROWS, cap * sh), 0)

    def landed(block, place):
        picks = jnp.where(row_ids == place[:, : cap * sh], 1.0, 0.0).astype(jnp.bfloat16)
        return jnp.dot(picks, block, preferred_element_type=jnp.float32)

    acc[...] = landed(send_x[0], send_m[0])

    def take_one(i, carry):
        step = jnp.where(i < tiles // 2, i, tiles - 1 - (i - tiles // 2))
        data_copy(step).wait_recv()
        place_copy(step).wait_recv()
        acc[...] += landed(recv_x[step], recv_m[step])
        return carry

    lax.fori_loop(1, tiles, take_one, 0)

    def part_copy(q):
        return pltpu.make_async_remote_copy(
            src_ref=part_s.at[q], dst_ref=part_r.at[q],
            send_sem=sp_sem.at[q], recv_sem=rp_sem.at[q],
            device_id=owner_id(q)[1], device_id_type=MESH,
        )

    for q in range(1, owners):
        peer = owner_id(q)[0]
        start = pl.multiple_of(peer * own_rows, own_rows)
        part_s[q] = acc[pl.ds(start, own_rows), :].astype(jnp.bfloat16)
        part_copy(q).start()
    start = pl.multiple_of(mine * own_rows, own_rows)
    total = acc[pl.ds(start, own_rows), :]
    for q in range(1, owners):
        part_copy(q).wait_recv()
        total = total + part_r[q].astype(jnp.float32)
    out[...] = total[:, :sw] / (total[:, sw:] + 1.0)

    def drain(step, carry):
        data_copy(step).wait_send()
        place_copy(step).wait_send()
        return carry

    lax.fori_loop(1, tiles, drain, 0)
    for q in range(1, owners):
        part_copy(q).wait_send()


def local(
    stamps, variance, basis_v, basis_u, coefficients, coef_index, tile_dest, row_offset, sub_pixel
):
    tiles = lax.axis_size("tile")
    rows_n = lax.axis_size("row")
    bands = lax.axis_size("band")
    count, sh, sw = stamps.shape
    nb = basis_v.shape[0]
    cap = max(2, (count + tiles - 1) // tiles)
    owners = rows_n * bands
    own_rows = TILE_ROWS // owners
    width = -(-cap * sh // 128) * 128
    vmem = pl.BlockSpec(memory_space=pltpu.VMEM)
    smem = pl.BlockSpec(memory_space=pltpu.SMEM)
    nb_pad = -(-nb // 8) * 8
    bf16, f32 = jnp.bfloat16, jnp.float32
    return pl.pallas_call(
        functools.partial(kernel, (tiles, rows_n, bands, cap)),
        out_shape=jax.ShapeDtypeStruct((own_rows, sw), f32),
        in_specs=[vmem] * 5 + [smem] * 4,
        out_specs=vmem,
        scratch_shapes=[
            pltpu.VMEM((nb_pad, sw), f32),
            pltpu.VMEM((nb_pad, sw), f32),
            pltpu.VMEM((nb * sh, sh), bf16),
            pltpu.VMEM((nb * sw, sw), bf16),
            pltpu.VMEM((cap * sh, nb * sw), bf16),
            pltpu.VMEM((tiles, cap * sh, 2 * sw), bf16),
            pltpu.VMEM((tiles, 1, width), jnp.int32),
            pltpu.VMEM((tiles, cap * sh, 2 * sw), bf16),
            pltpu.VMEM((tiles, 1, width), jnp.int32),
            pltpu.VMEM((TILE_ROWS, 2 * sw), f32),
            pltpu.VMEM((owners, own_rows, 2 * sw), bf16),
            pltpu.VMEM((owners, own_rows, 2 * sw), bf16),
            pltpu.SemaphoreType.DMA((tiles,)),
            pltpu.SemaphoreType.DMA((tiles,)),
            pltpu.SemaphoreType.DMA((tiles,)),
            pltpu.SemaphoreType.DMA((tiles,)),
            pltpu.SemaphoreType.DMA((owners,)),
            pltpu.SemaphoreType.DMA((owners,)),
        ],
        compiler_params=pltpu.CompilerParams(
            collective_id=0, has_side_effects=True, vmem_limit_bytes=48 * 1024 * 1024
        ),
    )(stamps, variance, basis_v, basis_u, coefficients, coef_index, tile_dest, row_offset, sub_pixel)


def solution(mesh):
    in_specs = (
        P(("patch", "tile", "row", "band"), None, None),
        P(("patch", "tile", "row", "band"), None, None),
        P(),
        P(),
        P("patch", None),
        P(("patch", "tile", "row", "band")),
        P(("patch", "tile", "row", "band")),
        P(("patch", "tile", "row", "band")),
        P(("patch", "tile", "row", "band"), None),
    )
    out_specs = P(("patch", "tile", "row", "band"), None)
    return jax.shard_map(local, mesh=mesh, in_specs=in_specs, out_specs=out_specs, check_vma=False)
```

time: 141 us -> 35.7 us (0.25); the launches traced: 139 us -> 35.5 us
  waiting for transfers between devices: 33.9 us -> 0 us
  Pallas kernels: 0 us -> 31 us
  other arithmetic: 26.9 us -> 0 us
  local copies, waits for them, and re-layouts: 28.8 us -> 4.39 us
  matrix products: 20.6 us -> 0 us
  starting transfers between devices: 15 us -> 0 us
  between operations: 13.6 us -> 0.08 us
    pallas_call x0 -> x1, Pallas kernels: none -> 31 us  [local(): pl.pallas_call(functools.partial(kernel, (tiles, rows_n, bands, cap)), ou...]
    dot_general x15 -> x0, matrix products: 20.6 us -> none  [the longest x6 9.64 us: one_group(): jnp.dot(flattened, horiz_table, preferred_element_type=jnp.float32)]
    scatter-add x2 -> x0, other arithmetic: 20 us -> none  [the longest x1 10.6 us: local(): numer_tile = jnp.zeros((TILE_ROWS, stamp_cols), jnp.float32).at[rows_flat...]
    all_to_all x3 -> x0, waiting for transfers between devices: 18.6 us -> none  [the longest x1 11.9 us: local(): lax.all_to_all(pack(variance), 'tile', split_axis=0, concat_axis=0, tiled...]
    reduce_scatter x2 -> x0, waiting for transfers between devices: 15.2 us -> none  [the longest x1 14 us: local(): lax.psum_scatter(denom_tile, ('row', 'band'), scatter_dimension=0, tiled=...]
    all_to_all x3 -> x0, starting transfers between devices: 14.9 us -> none  [the longest x1 6.33 us: local(): lax.all_to_all(pack(meta_sent), 'tile', split_axis=0, concat_axis=0, tile...]
    scatter x3 -> x0, local copies, waits for them, and re-layouts: 9.36 us -> none  [pack(): filled = empty_buffer.at[slot_of].set(values)]
    reshape x9 -> x0, local copies, waits for them, and re-layouts: 6.32 us -> none  [the longest x6 5.49 us: one_group(): horizontal = horizontal.reshape(group_size, stamp_rows, nbasis, stamp_cols)]
  transfers between devices with their start and end apart: 5 -> 0, of which waited for: 4 -> 0; matrix products, arithmetic and copies ran while one was open for 40% -> 0% of each run, Pallas kernels for 0% -> 0%
where the time goes in v1:
time: 35.7 us; the launch traced here: 35.5 us
  Pallas kernels  31 us (87%)
  local copies, waits for them, and re-layouts  4.39 us (12%)
    pallas_call x1, Pallas kernels, local(): pl.pallas_call(functools.partial(kernel, (tiles, rows_n, bands, cap)), ou...  31 us
    unnamed x17, local copies, waits for them, and re-layouts  4.39 us

profile of v1, /device:TPU:0, one launch (start us, length us, event | category | flops | bytes accessed | tf_op | source)
XLA Modules:
  0.0 35.5 jit_solution(9213967624637456780)
XLA Ops:
  0.0 0.8 %copy.11.sub_pixel = s32[24,2]{1,0:T(8,128)S(1)} copy(s32[24,2]{0,1:T(2,128)} %param.17) | data formatting | bytes 384 | tf_op args[8]
  0.8 0.0 copy-start.2
  0.8 0.0 copy-start.3
  0.8 0.0 copy-start.4
  0.8 0.0 copy-start.5
  0.8 0.0 copy-start.6
  0.8 1.0 %copy.10.coef = f32[400,21]{1,0:T(8,128)S(1)} copy(f32[400,21]{0,1:T(8,128)} %param.13) | data formatting | bytes 67200 | tf_op args[4]
  1.8 0.0 copy-done.2
  1.8 0.0 copy-done.3
  1.8 0.0 copy-done.4
  1.8 0.0 copy-done.5
  1.8 0.0 copy-done.6
  1.8 0.0 copy-start
  1.8 1.0 %copy-done = bf16[24,64,128]{2,1,0:T(8,128)(2,1)S(1)} copy-done((bf16[24,64,128]{2,1,0:T(8,128)(2,1)S(1)}, bf16[24,64,128]{2,1,0:T(8,128)(2,1)}, u32[]{:S(2)}) %copy-start) | copy-done | bytes 393240
  2.8 0.0 copy-start.1
  2.8 1.0 %copy-done.1 = bf16[24,64,128]{2,1,0:T(8,128)(2,1)S(1)} copy-done((bf16[24,64,128]{2,1,0:T(8,128)(2,1)S(1)}, bf16[24,64,128]{2,1,0:T(8,128)(2,1)}, u32[]{:S(2)}) %copy-start.1) | copy-done | bytes 393240
  3.8 31.0 %shard_map.91 = f32[256,128]{1,0:T(8,128)S(1)} custom-call(bf16[24,64,128]{2,1,0:T(8,128)(2,1)S(1)} %copy-done, bf16[24,64,128]{2,1,0:T(8,128)(2,1)S(1)} %copy-done.1, bf16[21,41]{1,0:T(8,128)(2,1)S(1)} %copy-done.2, bf16[21,41]{1,0:T(8,128)(2,1)S(1)} %copy-done.3, f32[400,21]{1,0:T(8,128)S(1)} %copy.10.coef, s32[24]{0:T(128)S(1)} %copy-done.4, ...), custom_call_target="tpu_custom_call" | custom-call | tf_op jit(solution)/shard_map/pallas_call | solution.py:215
  34.8 0.7 %copy.13 = f32[256,128]{1,0:T(8,128)} copy(f32[256,128]{1,0:T(8,128)S(1)} %shard_map.91) | data formatting | bytes 262144
Async XLA Ops:
  0.8 1.0 %copy-start.2 = (bf16[21,41]{1,0:T(8,128)(2,1)S(1)}, bf16[21,41]{1,0:T(8,128)(2,1)}, u32[]{:S(2)}) copy-start(bf16[21,41]{1,0:T(8,128)(2,1)} %basis_v.1) | copy-start | bytes 5170
  0.8 1.0 %copy-start.3 = (bf16[21,41]{1,0:T(8,128)(2,1)S(1)}, bf16[21,41]{1,0:T(8,128)(2,1)}, u32[]{:S(2)}) copy-start(bf16[21,41]{1,0:T(8,128)(2,1)} %basis_u.1) | copy-start | bytes 5170
  0.8 1.0 %copy-start.4 = (s32[24]{0:T(128)S(1)}, s32[24]{0:T(128)}, u32[]{:S(2)}) copy-start(s32[24]{0:T(128)} %coef_index.1) | copy-start | bytes 292
  0.8 1.0 %copy-start.5 = (s32[24]{0:T(128)S(1)}, s32[24]{0:T(128)}, u32[]{:S(2)}) copy-start(s32[24]{0:T(128)} %tile_dest.1) | copy-start | bytes 292
  0.8 1.0 %copy-start.6 = (s32[24]{0:T(128)S(1)}, s32[24]{0:T(128)}, u32[]{:S(2)}) copy-start(s32[24]{0:T(128)} %row_offset.1) | copy-start | bytes 292
  1.8 1.0 %copy-start = (bf16[24,64,128]{2,1,0:T(8,128)(2,1)S(1)}, bf16[24,64,128]{2,1,0:T(8,128)(2,1)}, u32[]{:S(2)}) copy-start(bf16[24,64,128]{2,1,0:T(8,128)(2,1)} %stamps.1) | copy-start | bytes 1179652
  2.8 1.0 %copy-start.1 = (bf16[24,64,128]{2,1,0:T(8,128)(2,1)S(1)}, bf16[24,64,128]{2,1,0:T(8,128)(2,1)}, u32[]{:S(2)}) copy-start(bf16[24,64,128]{2,1,0:T(8,128)(2,1)} %variance.1) | copy-start | bytes 1179652

commit v2 on v1

--- a/solution.py
+++ b/solution.py
@@ -29,11 +29,24 @@
 
 def kernel(
     sizes,
+    stamps_h, variance_h, basis_v_h, basis_u_h, coef_h, index_h, dest_h, offset_h, pixel_h,
+    out,
     stamps, variance, basis_v, basis_u, coef, coef_index, tile_dest, row_offset, sub_pixel,
-    out,
     taps_v, taps_u, vtab, utab, tmat, send_x, send_m, recv_x, recv_m, acc, part_s, part_r,
-    sx_sem, rx_sem, sm_sem, rm_sem, sp_sem, rp_sem,
+    in_sem, sx_sem, rx_sem, sm_sem, rm_sem, sp_sem, rp_sem,
 ):
+    loads = [
+        pltpu.make_async_copy(src, dst, in_sem.at[i])
+        for i, (src, dst) in enumerate(
+            [
+                (basis_v_h, basis_v), (basis_u_h, basis_u), (stamps_h, stamps), (coef_h, coef),
+                (dest_h, tile_dest), (index_h, coef_index), (offset_h, row_offset),
+                (pixel_h, sub_pixel), (variance_h, variance),
+            ]
+        )
+    ]
+    for load in loads:
+        load.start()
     tiles, rows_n, bands, cap = sizes
     count, sh, sw = stamps.shape
     nb, tap_count = basis_v.shape
@@ -55,12 +68,15 @@
     for q in range(1, owners):
         pl.semaphore_signal(barrier, inc=1, device_id=owner_id(q)[1], device_id_type=MESH)
 
-    taps_v[...] = jnp.zeros_like(taps_v)
-    taps_u[...] = jnp.zeros_like(taps_u)
-    taps_v[0:nb, 0:tap_count] = basis_v[...].astype(jnp.float32)
-    taps_u[0:nb, 0:tap_count] = basis_u[...].astype(jnp.float32)
-    taps_v[...] = pltpu.roll(taps_v[...], sw - half, 1)
-    taps_u[...] = pltpu.roll(taps_u[...], sw - half, 1)
+    tap_ids = lax.broadcasted_iota(jnp.int32, (tap_count, sw), 0)
+    lag_ids = lax.broadcasted_iota(jnp.int32, (tap_count, sw), 1)
+    lag_ids = jnp.where(lag_ids > half, lag_ids - sw, lag_ids)
+    forward = jnp.where(tap_ids == lag_ids + half, 1.0, 0.0).astype(jnp.bfloat16)
+    mirrored = jnp.where(tap_ids == half - lag_ids, 1.0, 0.0).astype(jnp.bfloat16)
+    loads[0].wait()
+    taps_v[...] = jnp.dot(basis_v[...], forward, preferred_element_type=jnp.float32)
+    loads[1].wait()
+    taps_u[...] = jnp.dot(basis_u[...], mirrored, preferred_element_type=jnp.float32)
     lag = lax.broadcasted_iota(jnp.int32, (sw, sw), 1) - lax.broadcasted_iota(jnp.int32, (sw, sw), 0)
     near = jnp.abs(lag) <= half
     for k in range(nb):
@@ -69,8 +85,10 @@
         vtab[k * sh : (k + 1) * sh, :] = rolled[:, :sh].astype(jnp.bfloat16)
         line = jnp.broadcast_to(taps_u[k : k + 1, :], (sw, sw))
         rolled = pltpu.roll(line, 0, 1, stride=1, stride_axis=0)
-        utab[k * sw : (k + 1) * sw, :] = jnp.where(near, rolled, 0.0).T.astype(jnp.bfloat16)
-
+        utab[k * sw : (k + 1) * sw, :] = jnp.where(near, rolled, 0.0).astype(jnp.bfloat16)
+
+    for load in loads[2:]:
+        load.wait()
     pl.semaphore_wait(barrier, tiles - 1 + owners - 1)
 
     last_row = lax.broadcasted_iota(jnp.int32, (sh, sw), 0) == sh - 1
@@ -78,6 +96,8 @@
     width = send_m.shape[2]
     lane = lax.broadcasted_iota(jnp.int32, (1, width), 1)
     chunk = largest_divisor(nb, 7)
+    digit_bits = count.bit_length()
+    exposure_ids = lax.broadcasted_iota(jnp.int32, coef.shape, 1)
 
     def bilinear(values, frac_rows, frac_cols):
         below = jnp.where(last_row, values, pltpu.roll(values, sh - 1, 0))
@@ -103,15 +123,18 @@
         dst = paired(me, step, tiles)
         listed = jnp.int32(0)
         for s in range(count):
-            listed = jnp.where(tile_dest[s] == dst, listed * (count + 1) + (s + 1), listed)
+            listed = jnp.where(tile_dest[s] == dst, (listed << digit_bits) + (s + 1), listed)
         picks, live = [], []
         for r in range(cap):
-            digit = lax.rem(listed, count + 1)
-            listed = lax.div(listed, count + 1)
+            digit = listed & ((1 << digit_bits) - 1)
+            listed = listed >> digit_bits
             picks.append(jnp.maximum(digit - 1, 0))
             live.append(digit > 0)
         images = jnp.concatenate([stamps[p] for p in picks], axis=1)
-        weights = [coef[pl.ds(coef_index[p], 1), :] for p in picks]
+        weights = [
+            jnp.sum(jnp.where(exposure_ids == coef_index[p], coef[...], 0.0), axis=1, keepdims=True)
+            for p in picks
+        ]
         for base in range(0, nb, chunk):
             part = jnp.dot(
                 vtab[base * sh : (base + chunk) * sh, :], images, preferred_element_type=jnp.float32
@@ -119,7 +142,7 @@
             for k in range(chunk):
                 for r in range(cap):
                     block = part[k * sh : (k + 1) * sh, r * sw : (r + 1) * sw]
-                    scale = weights[r][:, base + k : base + k + 1]
+                    scale = weights[r][base + k : base + k + 1, :]
                     tmat[r * sh : (r + 1) * sh, (base + k) * sw : (base + k + 1) * sw] = (
                         block * scale
                     ).astype(jnp.bfloat16)
@@ -128,8 +151,8 @@
         place = jnp.full((1, width), -1, jnp.int32)
         for r in range(cap):
             p = picks[r]
-            frac_rows = sub_pixel[p, 0].astype(jnp.float32) * (1.0 / SUBSTEPS)
-            frac_cols = sub_pixel[p, 1].astype(jnp.float32) * (1.0 / SUBSTEPS)
+            frac_rows = sub_pixel[0, p].astype(jnp.float32) * (1.0 / SUBSTEPS)
+            frac_cols = sub_pixel[1, p].astype(jnp.float32) * (1.0 / SUBSTEPS)
             warped = bilinear(matched[r * sh : (r + 1) * sh, :], frac_rows, frac_cols)
             spread = bilinear(variance[p].astype(jnp.float32), frac_rows, frac_cols)
             weight = 1.0 / spread
@@ -209,17 +232,21 @@
     own_rows = TILE_ROWS // owners
     width = -(-cap * sh // 128) * 128
     vmem = pl.BlockSpec(memory_space=pltpu.VMEM)
-    smem = pl.BlockSpec(memory_space=pltpu.SMEM)
-    nb_pad = -(-nb // 8) * 8
+    anywhere = pl.BlockSpec(memory_space=pl.ANY)
+    coefficients, sub_pixel = coefficients.T, sub_pixel.T
+    big = [stamps, variance, basis_v, basis_u, coefficients]
+    small = [coef_index, tile_dest, row_offset, sub_pixel]
     bf16, f32 = jnp.bfloat16, jnp.float32
     return pl.pallas_call(
         functools.partial(kernel, (tiles, rows_n, bands, cap)),
         out_shape=jax.ShapeDtypeStruct((own_rows, sw), f32),
-        in_specs=[vmem] * 5 + [smem] * 4,
+        in_specs=[anywhere] * 9,
         out_specs=vmem,
         scratch_shapes=[
-            pltpu.VMEM((nb_pad, sw), f32),
-            pltpu.VMEM((nb_pad, sw), f32),
+            *(pltpu.VMEM(x.shape, x.dtype) for x in big),
+            *(pltpu.SMEM(x.shape, x.dtype) for x in small),
+            pltpu.VMEM((nb, sw), f32),
+            pltpu.VMEM((nb, sw), f32),
             pltpu.VMEM((nb * sh, sh), bf16),
             pltpu.VMEM((nb * sw, sw), bf16),
             pltpu.VMEM((cap * sh, nb * sw), bf16),
@@ -230,6 +257,7 @@
             pltpu.VMEM((TILE_ROWS, 2 * sw), f32),
             pltpu.VMEM((owners, own_rows, 2 * sw), bf16),
             pltpu.VMEM((owners, own_rows, 2 * sw), bf16),
+            pltpu.SemaphoreType.DMA((9,)),
             pltpu.SemaphoreType.DMA((tiles,)),
             pltpu.SemaphoreType.DMA((tiles,)),
             pltpu.SemaphoreType.DMA((tiles,)),
@@ -238,9 +266,9 @@
             pltpu.SemaphoreType.DMA((owners,)),
         ],
         compiler_params=pltpu.CompilerParams(
-            collective_id=0, has_side_effects=True, vmem_limit_bytes=48 * 1024 * 1024
+            collective_id=0, has_side_effects=True, vmem_limit_bytes=56 * 1024 * 1024
         ),
-    )(stamps, variance, basis_v, basis_u, coefficients, coef_index, tile_dest, row_offset, sub_pixel)
+    )(*big, *small)
 
 
 def solution(mesh):

time: 35.7 us -> 32.4 us (0.908)
  local copies, waits for them, and re-layouts: 4.39 us -> 1.57 us
  Pallas kernels: 31 us -> 30.6 us
    unnamed x17 -> x1, local copies, waits for them, and re-layouts: 4.39 us -> 1.57 us
    pallas_call x1, Pallas kernels: 31 us -> 30.6 us  [local(): pl.pallas_call(functools.partial(kernel, (tiles, rows_n, bands, cap)), ou...]
where the time goes in v2:
time: 32.4 us; the launch traced here: 32.2 us
  Pallas kernels  30.6 us (94%)
  local copies, waits for them, and re-layouts  1.57 us (5%)
    pallas_call x1, Pallas kernels, local(): pl.pallas_call(functools.partial(kernel, (tiles, rows_n, bands, cap)), ou...  30.6 us
    unnamed x1, local copies, waits for them, and re-layouts  1.57 us

profile of v2, /device:TPU:0, one launch (start us, length us, event | category | flops | bytes accessed | tf_op | source)
XLA Modules:
  0.0 32.2 jit_solution(4706296382864912748)
XLA Ops:
  0.0 30.6 %shard_map.91 = f32[256,128]{1,0:T(8,128)} custom-call(bf16[24,64,128]{2,1,0:T(8,128)(2,1)} %stamps_h.1, bf16[24,64,128]{2,1,0:T(8,128)(2,1)} %variance_h.1, bf16[21,41]{1,0:T(8,128)(2,1)} %basis_v_h.1, bf16[21,41]{1,0:T(8,128)(2,1)} %basis_u_h.1, f32[21,400]{1,0:T(8,128)} %bitcast.2, s32[24]{0:T(128)} %index_h.1, s32[24]{0:T(128)} %dest_h.1, s32[24]{0:T(128)} %offset_h.1, ...), custom_call_target="tpu_custom_call" | custom-call | tf_op jit(solution)/shard_map/pallas_call | solution.py:240
  30.6 1.6 %copy.11 = f32[256,128]{1,0:T(8,128)} copy(f32[256,128]{1,0:T(8,128)} %shard_map.91) | data formatting | bytes 262144

commit v3 on v2

--- a/solution.py
+++ b/solution.py
@@ -27,47 +27,43 @@
     return total
 
 
-def kernel(
-    sizes,
-    stamps_h, variance_h, basis_v_h, basis_u_h, coef_h, index_h, dest_h, offset_h, pixel_h,
-    out,
-    stamps, variance, basis_v, basis_u, coef, coef_index, tile_dest, row_offset, sub_pixel,
-    taps_v, taps_u, vtab, utab, tmat, send_x, send_m, recv_x, recv_m, acc, part_s, part_r,
-    in_sem, sx_sem, rx_sem, sm_sem, rm_sem, sp_sem, rp_sem,
-):
-    loads = [
-        pltpu.make_async_copy(src, dst, in_sem.at[i])
-        for i, (src, dst) in enumerate(
-            [
-                (basis_v_h, basis_v), (basis_u_h, basis_u), (stamps_h, stamps), (coef_h, coef),
-                (dest_h, tile_dest), (index_h, coef_index), (offset_h, row_offset),
-                (pixel_h, sub_pixel), (variance_h, variance),
-            ]
-        )
-    ]
+def start_loads(sems, *pairs):
+    loads = [pltpu.make_async_copy(src, dst, sems.at[i]) for i, (src, dst) in enumerate(pairs)]
     for load in loads:
         load.start()
-    tiles, rows_n, bands, cap = sizes
-    count, sh, sw = stamps.shape
+    return loads
+
+
+def bilinear_of(sh, sw):
+    last_row = lax.broadcasted_iota(jnp.int32, (sh, sw), 0) == sh - 1
+    last_col = lax.broadcasted_iota(jnp.int32, (sh, sw), 1) == sw - 1
+
+    def bilinear(values, frac_rows, frac_cols):
+        below = jnp.where(last_row, values, pltpu.roll(values, sh - 1, 0))
+        mixed = (1.0 - frac_rows) * values + frac_rows * below
+        beside = jnp.where(last_col, mixed, pltpu.roll(mixed, sw - 1, 1))
+        return (1.0 - frac_cols) * mixed + frac_cols * beside
+
+    return bilinear
+
+
+def listed_stamps(tile_dest, dst, count, cap):
+    bits = count.bit_length()
+    listed = jnp.int32(0)
+    for s in range(count):
+        listed = jnp.where(tile_dest[s] == dst, (listed << bits) + (s + 1), listed)
+    picks, live = [], []
+    for r in range(cap):
+        digit = listed & ((1 << bits) - 1)
+        listed = listed >> bits
+        picks.append(jnp.maximum(digit - 1, 0))
+        live.append(digit > 0)
+    return picks, live
+
+
+def fill_tables(loads, basis_v, basis_u, taps_v, taps_u, vtab, utab, sh, sw):
     nb, tap_count = basis_v.shape
     half = (tap_count - 1) // 2
-    owners = rows_n * bands
-    own_rows = TILE_ROWS // owners
-    me = lax.axis_index("tile")
-    mine = lax.axis_index("row") * bands + lax.axis_index("band")
-
-    def owner_id(q):
-        peer = lax.rem(mine + q, owners)
-        return peer, {"row": lax.div(peer, bands), "band": lax.rem(peer, bands)}
-
-    barrier = pltpu.get_barrier_semaphore()
-    for step in range(1, tiles):
-        pl.semaphore_signal(
-            barrier, inc=1, device_id={"tile": lax.rem(me + step, tiles)}, device_id_type=MESH
-        )
-    for q in range(1, owners):
-        pl.semaphore_signal(barrier, inc=1, device_id=owner_id(q)[1], device_id_type=MESH)
-
     tap_ids = lax.broadcasted_iota(jnp.int32, (tap_count, sw), 0)
     lag_ids = lax.broadcasted_iota(jnp.int32, (tap_count, sw), 1)
     lag_ids = jnp.where(lag_ids > half, lag_ids - sw, lag_ids)
@@ -87,23 +83,52 @@
         rolled = pltpu.roll(line, 0, 1, stride=1, stride_axis=0)
         utab[k * sw : (k + 1) * sw, :] = jnp.where(near, rolled, 0.0).astype(jnp.bfloat16)
 
+
+def kernel(
+    sizes,
+    stamps_h, variance_h, basis_v_h, basis_u_h, coef_h, index_h, dest_h, offset_h, pixel_h,
+    out,
+    stamps, variance, basis_v, basis_u, coef, coef_index, tile_dest, row_offset, sub_pixel,
+    taps_v, taps_u, vtab, utab, tmat, send_x, send_m, recv_x, recv_m, acc, part_s, part_r,
+    in_sem, sx_sem, rx_sem, sm_sem, rm_sem, sp_sem, rp_sem,
+):
+    loads = start_loads(
+        in_sem,
+        (basis_v_h, basis_v), (basis_u_h, basis_u), (stamps_h, stamps), (coef_h, coef),
+        (dest_h, tile_dest), (index_h, coef_index), (offset_h, row_offset),
+        (pixel_h, sub_pixel), (variance_h, variance),
+    )
+    tiles, rows_n, bands, cap = sizes
+    count, sh, sw = stamps.shape
+    nb, tap_count = basis_v.shape
+    half = (tap_count - 1) // 2
+    owners = rows_n * bands
+    own_rows = TILE_ROWS // owners
+    me = lax.axis_index("tile")
+    mine = lax.axis_index("row") * bands + lax.axis_index("band")
+
+    def owner_id(q):
+        peer = lax.rem(mine + q, owners)
+        return peer, {"row": lax.div(peer, bands), "band": lax.rem(peer, bands)}
+
+    barrier = pltpu.get_barrier_semaphore()
+    for step in range(1, tiles):
+        pl.semaphore_signal(
+            barrier, inc=1, device_id={"tile": lax.rem(me + step, tiles)}, device_id_type=MESH
+        )
+    for q in range(1, owners):
+        pl.semaphore_signal(barrier, inc=1, device_id=owner_id(q)[1], device_id_type=MESH)
+
+    fill_tables(loads, basis_v, basis_u, taps_v, taps_u, vtab, utab, sh, sw)
     for load in loads[2:]:
         load.wait()
     pl.semaphore_wait(barrier, tiles - 1 + owners - 1)
 
-    last_row = lax.broadcasted_iota(jnp.int32, (sh, sw), 0) == sh - 1
-    last_col = lax.broadcasted_iota(jnp.int32, (sh, sw), 1) == sw - 1
+    bilinear = bilinear_of(sh, sw)
     width = send_m.shape[2]
     lane = lax.broadcasted_iota(jnp.int32, (1, width), 1)
     chunk = largest_divisor(nb, 7)
-    digit_bits = count.bit_length()
     exposure_ids = lax.broadcasted_iota(jnp.int32, coef.shape, 1)
-
-    def bilinear(values, frac_rows, frac_cols):
-        below = jnp.where(last_row, values, pltpu.roll(values, sh - 1, 0))
-        mixed = (1.0 - frac_rows) * values + frac_rows * below
-        beside = jnp.where(last_col, mixed, pltpu.roll(mixed, sw - 1, 1))
-        return (1.0 - frac_cols) * mixed + frac_cols * beside
 
     def data_copy(step):
         return pltpu.make_async_remote_copy(
@@ -121,15 +146,7 @@
 
     def produce(step):
         dst = paired(me, step, tiles)
-        listed = jnp.int32(0)
-        for s in range(count):
-            listed = jnp.where(tile_dest[s] == dst, (listed << digit_bits) + (s + 1), listed)
-        picks, live = [], []
-        for r in range(cap):
-            digit = listed & ((1 << digit_bits) - 1)
-            listed = listed >> digit_bits
-            picks.append(jnp.maximum(digit - 1, 0))
-            live.append(digit > 0)
+        picks, live = listed_stamps(tile_dest, dst, count, cap)
         images = jnp.concatenate([stamps[p] for p in picks], axis=1)
         weights = [
             jnp.sum(jnp.where(exposure_ids == coef_index[p], coef[...], 0.0), axis=1, keepdims=True)
@@ -219,6 +236,190 @@
         part_copy(q).wait_send()
 
 
+def paired_kernel(
+    sizes,
+    stamps_h, variance_h, basis_v_h, basis_u_h, coef_h, index_h, dest_h, offset_h, pixel_h,
+    out,
+    stamps, variance, basis_v, basis_u, coef, coef_index, tile_dest, row_offset, sub_pixel,
+    taps_v, taps_u, vtab, utab, tmat, send_x, send_m, recv_x, recv_m, sum_s, sum_r, acc,
+    part_s, part_r,
+    in_sem, sx_sem, rx_sem, sm_sem, rm_sem, ss_sem, rs_sem, sp_sem, rp_sem,
+):
+    tiles, cap = sizes
+    count, sh, sw = stamps.shape
+    nb, tap_count = basis_v.shape
+    half = (tap_count - 1) // 2
+    pairs = tiles // 2
+    own_rows = TILE_ROWS // 2
+    rows = cap * sh
+    me = lax.axis_index("tile")
+    side = lax.axis_index("row") + lax.axis_index("band")
+    group, core = lax.div(me, 2), lax.rem(me, 2)
+    row_many = lax.axis_size("row") == 2
+
+    def position(dx, dc):
+        other = lax.rem(side + dx, 2)
+        spot = {"tile": group * 2 + lax.rem(core + dc, 2)}
+        spot["row" if row_many else "band"] = other
+        return spot
+
+    def far(step):
+        return {"tile": paired(group, step, pairs) * 2 + core}
+
+    loads = start_loads(
+        in_sem,
+        (basis_v_h, basis_v), (basis_u_h, basis_u), (stamps_h, stamps), (coef_h, coef),
+        (dest_h, tile_dest), (index_h, coef_index), (offset_h, row_offset),
+        (pixel_h, sub_pixel), (variance_h, variance),
+    )
+    slots = [(dx, dc) for dx in range(2) for dc in range(2)]
+    barrier = pltpu.get_barrier_semaphore()
+    for dx, dc in slots[1:]:
+        pl.semaphore_signal(barrier, inc=1, device_id=position(dx, dc), device_id_type=MESH)
+    for step in range(1, pairs):
+        pl.semaphore_signal(barrier, inc=1, device_id=far(step), device_id_type=MESH)
+
+    fill_tables(loads, basis_v, basis_u, taps_v, taps_u, vtab, utab, sh, sw)
+    for load in loads[2:]:
+        load.wait()
+
+    width = send_m.shape[3]
+    lane = lax.broadcasted_iota(jnp.int32, (1, width), 1)
+    chunk = largest_divisor(nb, 7)
+    exposure_ids = lax.broadcasted_iota(jnp.int32, coef.shape, 1)
+    bilinear = bilinear_of(sh, sw)
+
+    def group_copy(step, q):
+        return pltpu.make_async_remote_copy(
+            src_ref=send_x.at[step, q], dst_ref=recv_x.at[step, q],
+            send_sem=sx_sem.at[step, q], recv_sem=rx_sem.at[step, q],
+            device_id=position(*slots[q]), device_id_type=MESH,
+        )
+
+    def place_copy(step, q):
+        return pltpu.make_async_remote_copy(
+            src_ref=send_m.at[step, slots[q][1]], dst_ref=recv_m.at[step, q],
+            send_sem=sm_sem.at[step, q], recv_sem=rm_sem.at[step, q],
+            device_id=position(*slots[q]), device_id_type=MESH,
+        )
+
+    def sum_copy(step):
+        return pltpu.make_async_remote_copy(
+            src_ref=sum_s.at[step], dst_ref=sum_r.at[step],
+            send_sem=ss_sem.at[step], recv_sem=rs_sem.at[step],
+            device_id=far(step), device_id_type=MESH,
+        )
+
+    def produce(step):
+        base_tile = paired(group, step, pairs) * 2
+        picks, live = [], []
+        for dc in range(2):
+            more, alive = listed_stamps(tile_dest, base_tile + lax.rem(core + dc, 2), count, cap)
+            picks += more
+            live += alive
+        images = jnp.concatenate([stamps[p] for p in picks], axis=1)
+        weights = [
+            jnp.sum(jnp.where(exposure_ids == coef_index[p], coef[...], 0.0), axis=1, keepdims=True)
+            for p in picks
+        ]
+        for base in range(0, nb, chunk):
+            part = jnp.dot(
+                vtab[base * sh : (base + chunk) * sh, :], images, preferred_element_type=jnp.float32
+            )
+            for k in range(chunk):
+                for r in range(2 * cap):
+                    block = part[k * sh : (k + 1) * sh, r * sw : (r + 1) * sw]
+                    tmat[r * sh : (r + 1) * sh, (base + k) * sw : (base + k + 1) * sw] = (
+                        block * weights[r][base + k : base + k + 1, :]
+                    ).astype(jnp.bfloat16)
+        matched = jnp.dot(tmat[...], utab[...], preferred_element_type=jnp.float32)
+        matched = matched.astype(jnp.bfloat16).astype(jnp.float32)
+        for dc in range(2):
+            place = jnp.full((1, width), -1, jnp.int32)
+            for r in range(cap):
+                slot = dc * cap + r
+                p = picks[slot]
+                frac_rows = sub_pixel[0, p].astype(jnp.float32) * (1.0 / SUBSTEPS)
+                frac_cols = sub_pixel[1, p].astype(jnp.float32) * (1.0 / SUBSTEPS)
+                warped = bilinear(matched[slot * sh : (slot + 1) * sh, :], frac_rows, frac_cols)
+                spread = bilinear(variance[p].astype(jnp.float32), frac_rows, frac_cols)
+                weight = 1.0 / spread
+                numer = weight * warped
+                here = jnp.where(side == 0, numer, weight).astype(jnp.bfloat16)
+                there = jnp.where(side == 0, weight, numer).astype(jnp.bfloat16)
+                if dc == 0:
+                    recv_x[step, 0, r * sh : (r + 1) * sh, :] = here
+                else:
+                    send_x[step, 1, r * sh : (r + 1) * sh, :] = here
+                send_x[step, 2 + dc, r * sh : (r + 1) * sh, :] = there
+                first = jnp.where(live[slot], row_offset[p], -4 * TILE_ROWS)
+                inside = (lane >= r * sh) & (lane < (r + 1) * sh)
+                place = jnp.where(inside, first + lane - r * sh, place)
+            send_m[step, dc] = place
+            if dc == 0:
+                recv_m[step, 0] = place
+
+    def send_group(step):
+        for q in (2, 3, 1):
+            group_copy(step, q).start()
+            place_copy(step, q).start()
+
+    row_ids = lax.broadcasted_iota(jnp.int32, (TILE_ROWS, rows), 0)
+
+    def gathered(step):
+        total = None
+        for q in (0, 1, 2, 3):
+            if q > 0:
+                group_copy(step, q).wait_recv()
+                place_copy(step, q).wait_recv()
+            place = recv_m[step, q]
+            hit = jnp.where(row_ids == place[:, :rows], 1.0, 0.0).astype(jnp.bfloat16)
+            part = jnp.dot(hit, recv_x[step, q], preferred_element_type=jnp.float32)
+            total = part if total is None else total + part
+        return total
+
+    produce(pairs - 1)
+    pl.semaphore_wait(barrier, len(slots) - 1 + pairs - 1)
+    send_group(pairs - 1)
+
+    def one_step(i, carry):
+        step = pairs - 1 - i
+        produce(step)
+        send_group(step)
+        sum_s[step + 1] = gathered(step + 1).astype(jnp.bfloat16)
+        sum_copy(step + 1).start()
+        return carry
+
+    lax.fori_loop(1, pairs, one_step, 0)
+    acc[...] = gathered(0)
+    for step in range(1, pairs):
+        sum_copy(step).wait_recv()
+        acc[...] += sum_r[step].astype(jnp.float32)
+
+    part_copy = pltpu.make_async_remote_copy(
+        src_ref=part_s, dst_ref=part_r, send_sem=sp_sem.at[0], recv_sem=rp_sem.at[0],
+        device_id=position(1, 0), device_id_type=MESH,
+    )
+    start = pl.multiple_of((1 - side) * own_rows, own_rows)
+    part_s[...] = acc[pl.ds(start, own_rows), :].astype(jnp.bfloat16)
+    part_copy.start()
+    own = acc[pl.ds(pl.multiple_of(side * own_rows, own_rows), own_rows), :]
+    part_copy.wait_recv()
+    other = part_r[...].astype(jnp.float32)
+    out[...] = jnp.where(side == 0, own, other) / (jnp.where(side == 0, other, own) + 1.0)
+
+    def drain(step, carry):
+        for q in (1, 2, 3):
+            group_copy(step, q).wait_send()
+            place_copy(step, q).wait_send()
+        return carry
+
+    lax.fori_loop(0, pairs, drain, 0)
+    for step in range(1, pairs):
+        sum_copy(step).wait_send()
+    part_copy.wait_send()
+
+
 def local(
     stamps, variance, basis_v, basis_u, coefficients, coef_index, tile_dest, row_offset, sub_pixel
 ):
@@ -236,19 +437,53 @@
     coefficients, sub_pixel = coefficients.T, sub_pixel.T
     big = [stamps, variance, basis_v, basis_u, coefficients]
     small = [coef_index, tile_dest, row_offset, sub_pixel]
-    bf16, f32 = jnp.bfloat16, jnp.float32
+    bf16, f32, dma = jnp.bfloat16, jnp.float32, pltpu.SemaphoreType.DMA
+    inputs = [
+        *(pltpu.VMEM(x.shape, x.dtype) for x in big),
+        *(pltpu.SMEM(x.shape, x.dtype) for x in small),
+        pltpu.VMEM((nb, sw), f32),
+        pltpu.VMEM((nb, sw), f32),
+        pltpu.VMEM((nb * sh, sh), bf16),
+        pltpu.VMEM((nb * sw, sw), bf16),
+    ]
+    params = pltpu.CompilerParams(
+        collective_id=0, has_side_effects=True, vmem_limit_bytes=56 * 1024 * 1024
+    )
+    if owners == 2 and tiles % 2 == 0 and tiles > 2:
+        pairs = tiles // 2
+        return pl.pallas_call(
+            functools.partial(paired_kernel, (tiles, cap)),
+            out_shape=jax.ShapeDtypeStruct((own_rows, sw), f32),
+            in_specs=[anywhere] * 9,
+            out_specs=vmem,
+            scratch_shapes=[
+                *inputs,
+                pltpu.VMEM((2 * cap * sh, nb * sw), bf16),
+                pltpu.VMEM((pairs, 4, cap * sh, sw), bf16),
+                pltpu.VMEM((pairs, 2, 1, width), jnp.int32),
+                pltpu.VMEM((pairs, 4, cap * sh, sw), bf16),
+                pltpu.VMEM((pairs, 4, 1, width), jnp.int32),
+                pltpu.VMEM((pairs, TILE_ROWS, sw), bf16),
+                pltpu.VMEM((pairs, TILE_ROWS, sw), bf16),
+                pltpu.VMEM((TILE_ROWS, sw), f32),
+                pltpu.VMEM((own_rows, sw), bf16),
+                pltpu.VMEM((own_rows, sw), bf16),
+                dma((9,)),
+                *(dma((pairs, 4)) for _ in range(4)),
+                dma((pairs,)),
+                dma((pairs,)),
+                dma((1,)),
+                dma((1,)),
+            ],
+            compiler_params=params,
+        )(*big, *small)
     return pl.pallas_call(
         functools.partial(kernel, (tiles, rows_n, bands, cap)),
         out_shape=jax.ShapeDtypeStruct((own_rows, sw), f32),
         in_specs=[anywhere] * 9,
         out_specs=vmem,
         scratch_shapes=[
-            *(pltpu.VMEM(x.shape, x.dtype) for x in big),
-            *(pltpu.SMEM(x.shape, x.dtype) for x in small),
-            pltpu.VMEM((nb, sw), f32),
-            pltpu.VMEM((nb, sw), f32),
-            pltpu.VMEM((nb * sh, sh), bf16),
-            pltpu.VMEM((nb * sw, sw), bf16),
+            *inputs,
             pltpu.VMEM((cap * sh, nb * sw), bf16),
             pltpu.VMEM((tiles, cap * sh, 2 * sw), bf16),
             pltpu.VMEM((tiles, 1, width), jnp.int32),
@@ -265,9 +500,7 @@
             pltpu.SemaphoreType.DMA((owners,)),
             pltpu.SemaphoreType.DMA((owners,)),
         ],
-        compiler_params=pltpu.CompilerParams(
-            collective_id=0, has_side_effects=True, vmem_limit_bytes=56 * 1024 * 1024
-        ),
+        compiler_params=params,
     )(*big, *small)
 
 

time: 32.4 us -> 30.2 us (0.932)
  Pallas kernels: 30.6 us -> 28.5 us
    pallas_call x1, Pallas kernels: 30.6 us -> 28.5 us  [local(): pl.pallas_call(functools.partial(paired_kernel, (tiles, cap)), out_shape=...]
where the time goes in v3:
time: 30.2 us; the launch traced here: 30 us
  Pallas kernels  28.5 us (94%)
  local copies, waits for them, and re-layouts  1.57 us (5%)
    pallas_call x1, Pallas kernels, local(): pl.pallas_call(functools.partial(paired_kernel, (tiles, cap)), out_shape=...  28.5 us
    unnamed x1, local copies, waits for them, and re-layouts  1.57 us

profile of v3, /device:TPU:0, one launch (start us, length us, event | category | flops | bytes accessed | tf_op | source)
XLA Modules:
  0.0 30.0 jit_solution(13960351627678382257)
XLA Ops:
  0.0 28.5 %shard_map.91 = f32[256,128]{1,0:T(8,128)} custom-call(bf16[24,64,128]{2,1,0:T(8,128)(2,1)} %stamps_h.1, bf16[24,64,128]{2,1,0:T(8,128)(2,1)} %variance_h.1, bf16[21,41]{1,0:T(8,128)(2,1)} %basis_v_h.1, bf16[21,41]{1,0:T(8,128)(2,1)} %basis_u_h.1, f32[21,400]{1,0:T(8,128)} %bitcast.2, s32[24]{0:T(128)} %index_h.1, s32[24]{0:T(128)} %dest_h.1, s32[24]{0:T(128)} %offset_h.1, ...), custom_call_target="tpu_custom_call" | custom-call | tf_op jit(solution)/shard_map/pallas_call | solution.py:454
  28.5 1.6 %copy.11 = f32[256,128]{1,0:T(8,128)} copy(f32[256,128]{1,0:T(8,128)} %shard_map.91) | data formatting | bytes 262144

commit v4 on v3

--- a/solution.py
+++ b/solution.py
@@ -285,7 +285,7 @@
 
     width = send_m.shape[3]
     lane = lax.broadcasted_iota(jnp.int32, (1, width), 1)
-    chunk = largest_divisor(nb, 7)
+    chunk = largest_divisor(nb, 3)
     exposure_ids = lax.broadcasted_iota(jnp.int32, coef.shape, 1)
     bilinear = bilinear_of(sh, sw)
 
@@ -322,7 +322,16 @@
             jnp.sum(jnp.where(exposure_ids == coef_index[p], coef[...], 0.0), axis=1, keepdims=True)
             for p in picks
         ]
+        def across(first, last):
+            return jnp.dot(
+                tmat[:, first * sw : last * sw],
+                utab[first * sw : last * sw, :],
+                preferred_element_type=jnp.float32,
+            )
+
+        matched, done = None, 0
         for base in range(0, nb, chunk):
+            ready = base - base % (2 * chunk)
             part = jnp.dot(
                 vtab[base * sh : (base + chunk) * sh, :], images, preferred_element_type=jnp.float32
             )
@@ -332,10 +341,15 @@
                     tmat[r * sh : (r + 1) * sh, (base + k) * sw : (base + k + 1) * sw] = (
                         block * weights[r][base + k : base + k + 1, :]
                     ).astype(jnp.bfloat16)
-        matched = jnp.dot(tmat[...], utab[...], preferred_element_type=jnp.float32)
+            if ready > done:
+                term = across(done, ready)
+                matched = term if matched is None else matched + term
+                done = ready
+        term = across(done, nb)
+        matched = term if matched is None else matched + term
         matched = matched.astype(jnp.bfloat16).astype(jnp.float32)
         for dc in range(2):
-            place = jnp.full((1, width), -1, jnp.int32)
+            place = jnp.full((1, width), -4 * TILE_ROWS, jnp.int32)
             for r in range(cap):
                 slot = dc * cap + r
                 p = picks[slot]
@@ -364,7 +378,10 @@
             group_copy(step, q).start()
             place_copy(step, q).start()
 
-    row_ids = lax.broadcasted_iota(jnp.int32, (TILE_ROWS, rows), 0)
+    middle = TILE_ROWS // 2
+    row_ids = lax.broadcasted_iota(jnp.int32, (TILE_ROWS, rows), 0) - middle
+    row_ids = row_ids.astype(jnp.float32).astype(jnp.bfloat16)
+    one, zero = jnp.bfloat16(1.0), jnp.bfloat16(0.0)
 
     def gathered(step):
         total = None
@@ -372,8 +389,8 @@
             if q > 0:
                 group_copy(step, q).wait_recv()
                 place_copy(step, q).wait_recv()
-            place = recv_m[step, q]
-            hit = jnp.where(row_ids == place[:, :rows], 1.0, 0.0).astype(jnp.bfloat16)
+            place = (recv_m[step, q] - middle).astype(jnp.float32).astype(jnp.bfloat16)
+            hit = jnp.where(row_ids == place[:, :rows], one, zero)
             part = jnp.dot(hit, recv_x[step, q], preferred_element_type=jnp.float32)
             total = part if total is None else total + part
         return total

time: 30.2 us -> 29.9 us (0.990)
  Pallas kernels: 28.5 us -> 28.1 us
    pallas_call x1, Pallas kernels: 28.5 us -> 28.1 us  [local(): pl.pallas_call(functools.partial(paired_kernel, (tiles, cap)), out_shape=...]
where the time goes in v4:
time: 29.9 us; the launch traced here: 29.7 us
  Pallas kernels  28.1 us (94%)
  local copies, waits for them, and re-layouts  1.57 us (5%)
    pallas_call x1, Pallas kernels, local(): pl.pallas_call(functools.partial(paired_kernel, (tiles, cap)), out_shape=...  28.1 us
    unnamed x1, local copies, waits for them, and re-layouts  1.57 us

profile of v4, /device:TPU:0, one launch (start us, length us, event | category | flops | bytes accessed | tf_op | source)
XLA Modules:
  0.0 29.7 jit_solution(12261336984691350198)
XLA Ops:
  0.0 28.1 %shard_map.91 = f32[256,128]{1,0:T(8,128)} custom-call(bf16[24,64,128]{2,1,0:T(8,128)(2,1)} %stamps_h.1, bf16[24,64,128]{2,1,0:T(8,128)(2,1)} %variance_h.1, bf16[21,41]{1,0:T(8,128)(2,1)} %basis_v_h.1, bf16[21,41]{1,0:T(8,128)(2,1)} %basis_u_h.1, f32[21,400]{1,0:T(8,128)} %bitcast.2, s32[24]{0:T(128)} %index_h.1, s32[24]{0:T(128)} %dest_h.1, s32[24]{0:T(128)} %offset_h.1, ...), custom_call_target="tpu_custom_call" | custom-call | tf_op jit(solution)/shard_map/pallas_call | solution.py:471
  28.1 1.6 %copy.11 = f32[256,128]{1,0:T(8,128)} copy(f32[256,128]{1,0:T(8,128)} %shard_map.91) | data formatting | bytes 262144

commit v5 on v4

--- a/solution.py
+++ b/solution.py
@@ -242,8 +242,7 @@
     out,
     stamps, variance, basis_v, basis_u, coef, coef_index, tile_dest, row_offset, sub_pixel,
     taps_v, taps_u, vtab, utab, tmat, send_x, send_m, recv_x, recv_m, sum_s, sum_r, acc,
-    part_s, part_r,
-    in_sem, sx_sem, rx_sem, sm_sem, rm_sem, ss_sem, rs_sem, sp_sem, rp_sem,
+    in_sem, sx_sem, rx_sem, sm_sem, rm_sem, ss_sem, rs_sem,
 ):
     tiles, cap = sizes
     count, sh, sw = stamps.shape
@@ -263,8 +262,10 @@
         spot["row" if row_many else "band"] = other
         return spot
 
-    def far(step):
-        return {"tile": paired(group, step, pairs) * 2 + core}
+    def far(step, dx):
+        spot = {"tile": paired(group, step, pairs) * 2 + core}
+        spot["row" if row_many else "band"] = lax.rem(side + dx, 2)
+        return spot
 
     loads = start_loads(
         in_sem,
@@ -277,7 +278,8 @@
     for dx, dc in slots[1:]:
         pl.semaphore_signal(barrier, inc=1, device_id=position(dx, dc), device_id_type=MESH)
     for step in range(1, pairs):
-        pl.semaphore_signal(barrier, inc=1, device_id=far(step), device_id_type=MESH)
+        for dx in range(2):
+            pl.semaphore_signal(barrier, inc=1, device_id=far(step, dx), device_id_type=MESH)
 
     fill_tables(loads, basis_v, basis_u, taps_v, taps_u, vtab, utab, sh, sw)
     for load in loads[2:]:
@@ -303,12 +305,19 @@
             device_id=position(*slots[q]), device_id_type=MESH,
         )
 
-    def sum_copy(step):
+    def sum_copy(step, dx):
         return pltpu.make_async_remote_copy(
-            src_ref=sum_s.at[step], dst_ref=sum_r.at[step],
-            send_sem=ss_sem.at[step], recv_sem=rs_sem.at[step],
-            device_id=far(step), device_id_type=MESH,
-        )
+            src_ref=sum_s.at[step, dx], dst_ref=sum_r.at[step, dx],
+            send_sem=ss_sem.at[step, dx], recv_sem=rs_sem.at[step, dx],
+            device_id=far(step, dx), device_id_type=MESH,
+        )
+
+    def send_sums(step):
+        acc[...] = gathered(step)
+        for dx in (1, 0):
+            start = pl.multiple_of(lax.rem(side + dx, 2) * own_rows, own_rows)
+            sum_s[step, dx] = acc[pl.ds(start, own_rows), :].astype(jnp.bfloat16)
+            sum_copy(step, dx).start()
 
     def produce(step):
         base_tile = paired(group, step, pairs) * 2
@@ -396,33 +405,29 @@
         return total
 
     produce(pairs - 1)
-    pl.semaphore_wait(barrier, len(slots) - 1 + pairs - 1)
+    pl.semaphore_wait(barrier, len(slots) - 1 + 2 * (pairs - 1))
     send_group(pairs - 1)
 
     def one_step(i, carry):
         step = pairs - 1 - i
         produce(step)
         send_group(step)
-        sum_s[step + 1] = gathered(step + 1).astype(jnp.bfloat16)
-        sum_copy(step + 1).start()
+        send_sums(step + 1)
         return carry
 
     lax.fori_loop(1, pairs, one_step, 0)
     acc[...] = gathered(0)
-    for step in range(1, pairs):
-        sum_copy(step).wait_recv()
-        acc[...] += sum_r[step].astype(jnp.float32)
-
-    part_copy = pltpu.make_async_remote_copy(
-        src_ref=part_s, dst_ref=part_r, send_sem=sp_sem.at[0], recv_sem=rp_sem.at[0],
-        device_id=position(1, 0), device_id_type=MESH,
-    )
     start = pl.multiple_of((1 - side) * own_rows, own_rows)
-    part_s[...] = acc[pl.ds(start, own_rows), :].astype(jnp.bfloat16)
-    part_copy.start()
+    sum_s[0, 1] = acc[pl.ds(start, own_rows), :].astype(jnp.bfloat16)
+    sum_copy(0, 1).start()
     own = acc[pl.ds(pl.multiple_of(side * own_rows, own_rows), own_rows), :]
-    part_copy.wait_recv()
-    other = part_r[...].astype(jnp.float32)
+    other = jnp.zeros_like(own)
+    for step in range(pairs):
+        if step > 0:
+            sum_copy(step, 0).wait_recv()
+            own = own + sum_r[step, 0].astype(jnp.float32)
+        sum_copy(step, 1).wait_recv()
+        other = other + sum_r[step, 1].astype(jnp.float32)
     out[...] = jnp.where(side == 0, own, other) / (jnp.where(side == 0, other, own) + 1.0)
 
     def drain(step, carry):
@@ -432,9 +437,9 @@
         return carry
 
     lax.fori_loop(0, pairs, drain, 0)
-    for step in range(1, pairs):
-        sum_copy(step).wait_send()
-    part_copy.wait_send()
+    for step in range(pairs):
+        for dx in range(0 if step else 1, 2):
+            sum_copy(step, dx).wait_send()
 
 
 def local(
@@ -480,17 +485,13 @@
                 pltpu.VMEM((pairs, 2, 1, width), jnp.int32),
                 pltpu.VMEM((pairs, 4, cap * sh, sw), bf16),
                 pltpu.VMEM((pairs, 4, 1, width), jnp.int32),
-                pltpu.VMEM((pairs, TILE_ROWS, sw), bf16),
-                pltpu.VMEM((pairs, TILE_ROWS, sw), bf16),
+                pltpu.VMEM((pairs, 2, own_rows, sw), bf16),
+                pltpu.VMEM((pairs, 2, own_rows, sw), bf16),
                 pltpu.VMEM((TILE_ROWS, sw), f32),
-                pltpu.VMEM((own_rows, sw), bf16),
-                pltpu.VMEM((own_rows, sw), bf16),
                 dma((9,)),
                 *(dma((pairs, 4)) for _ in range(4)),
-                dma((pairs,)),
-                dma((pairs,)),
-                dma((1,)),
-                dma((1,)),
+                dma((pairs, 2)),
+                dma((pairs, 2)),
             ],
             compiler_params=params,
         )(*big, *small)

time: 29.9 us -> 27.6 us (0.923)
  Pallas kernels: 28.1 us -> 25.9 us
    pallas_call x1, Pallas kernels: 28.1 us -> 25.9 us  [local(): pl.pallas_call(functools.partial(paired_kernel, (tiles, cap)), out_shape=...]
where the time goes in v5:
time: 27.6 us; the launch traced here: 27.4 us
  Pallas kernels  25.9 us (94%)
  local copies, waits for them, and re-layouts  1.57 us (6%)
    pallas_call x1, Pallas kernels, local(): pl.pallas_call(functools.partial(paired_kernel, (tiles, cap)), out_shape=...  25.9 us
    unnamed x1, local copies, waits for them, and re-layouts  1.57 us

profile of v5, /device:TPU:0, one launch (start us, length us, event | category | flops | bytes accessed | tf_op | source)
XLA Modules:
  0.0 27.4 jit_solution(4499835279669851971)
XLA Ops:
  0.0 25.9 %shard_map.91 = f32[256,128]{1,0:T(8,128)} custom-call(bf16[24,64,128]{2,1,0:T(8,128)(2,1)} %stamps_h.1, bf16[24,64,128]{2,1,0:T(8,128)(2,1)} %variance_h.1, bf16[21,41]{1,0:T(8,128)(2,1)} %basis_v_h.1, bf16[21,41]{1,0:T(8,128)(2,1)} %basis_u_h.1, f32[21,400]{1,0:T(8,128)} %bitcast.2, s32[24]{0:T(128)} %index_h.1, s32[24]{0:T(128)} %dest_h.1, s32[24]{0:T(128)} %offset_h.1, ...), custom_call_target="tpu_custom_call" | custom-call | tf_op jit(solution)/shard_map/pallas_call | solution.py:476
  25.9 1.6 %copy.11 = f32[256,128]{1,0:T(8,128)} copy(f32[256,128]{1,0:T(8,128)} %shard_map.91) | data formatting | bytes 262144
